TPU v7x, 32 devices: a whole 2x2x4 slice. The times are simulated.
32 devices in a mesh: region: 2 (over y), cell: 16 (over z, x, core).
Axes of the slice: x: 2, y: 2, z: 4, core: 2. Of those that a mesh axis runs over, the one named last changes fastest.
Arguments:
- position: float32 [3, 256, 128], P(None, ('region', 'cell')), may hold values from 0 to 1
- velocity: float32 [3, 256, 128], P(None, ('region', 'cell')), may hold values from -6 to 6
- smoothing: float32 [256, 128], P(('region', 'cell')), may hold values from 0.3 to 0.5
- particle_mass: float32 [256, 128], P(('region', 'cell')), may hold values from 0.004 to 0.012
- energy: float32 [256, 128], P(('region', 'cell')), may hold values from 0.5 to 2
- density_old: float32 [256, 128], P(('region', 'cell')), may hold values from 0.3 to 1.2
- cell_count: int32 [256], P(('region', 'cell')), may hold values from 8 to 128, as said below
- active: int32 [256, 128], P(('region', 'cell')), may hold values from 0 to 1, as said below
- time_bin: int32 [256, 128], P(('region', 'cell')), may hold values from 0 to 5
- pair_source: int32 [256, 27], P(('region', 'cell')), may hold values from 0 to 41, as said below
- pair_shift: int32 [256, 27], P(('region', 'cell')), may hold values from 0 to 26, as said below
- export: int32 [512, 2], P(('region', 'cell')), may hold values from 0 to 7
Outputs:
- density: float32 [256, 128], P(('region', 'cell'))
- acceleration: float32 [3, 256, 128], P(None, ('region', 'cell'))
- kicked_velocity: float32 [3, 256, 128], P(None, ('region', 'cell'))
Inputs may be any that keep to these rules, and one draw needn't show every extreme that they name: `cell_count`: every device has a cell of exactly 128 particles. `active`: 0 in the slots past a cell's count. `pair_source`: pair 0 of a device's cell k names source k; a device's pairs name every one of its 42 sources. `pair_shift`: pair 0 has code 13; a cell's 27 codes are distinct.
All inputs are finite; a program needn't handle non-finite values.
Results may differ from a plain program's by a relative error of at most 0.0003.
Values sent between devices are 32-bit elements; how exact they have to be, the bound alone decides.
No kernel may reach another device: no remote copies, remote signals or barrier semaphores. Data moves between devices by JAX's collectives and lax.ppermute only.
A program may use at most 64 MiB of HBM per device.

v0:
```python
import functools
import math

import jax
import jax.numpy as jnp
from jax import lax
from jax.experimental import pallas as pl
from jax.experimental.pallas import tpu as pltpu
from jax.sharding import PartitionSpec as P

ADIABATIC = 5.0 / 3.0
STEP_MAX = 0.2
LANES = 128
ROWS = 8
FORCE_UNROLL = 7
PAIR_ROWS = 32
FAR_AWAY = 1e9
SPARE = FORCE_UNROLL

X, Y, Z, MASS, VX, VY, VZ, WIDE = range(ROWS)
SPREAD = (X, Y, Z, WIDE)
HEAT, DENS, LIVE = range(3)
SENT = 4
SPEED = 40.0
ACTIVE, STEP = SENT, SENT + 1
S_HEAT, S_RANK, S_REACH, S_CHOSEN = range(ROWS, ROWS + 4)
S_LOW, S_HIGH, S_ROWS = 2 * ROWS, 3 * ROWS, 4 * ROWS
F_RANK, F_ACTIVE, F_STEP, F_VX, F_VY, F_VZ, F_DENS = range(7)
DENS4, PRESS, INV6, HALF, SOUND = range(5)


def lane_gather(values, index):
    return jnp.take_along_axis(values, index, axis=1, mode="promise_in_bounds")


def lanes_of(shape):
    return lax.broadcasted_iota(jnp.int32, shape, len(shape) - 1)


def start_copies(arrays, landed, sem):
    copies = [
        pltpu.make_async_copy(array, place, sem.at[index])
        for index, (array, place) in enumerate(zip(arrays, landed))
    ]
    for copy in copies:
        copy.start()
    return copies


def pack_kernel(*refs):
    arrays, (own, outgoing, border) = refs[:10], refs[10:13]
    landed, sem = refs[13:-1], refs[-1]
    for copy in start_copies(arrays, landed, sem):
        copy.wait()
    count, export, position, velocity, smoothing, mass, energy, density_old, active, time_bin = landed
    cells = smoothing.shape[0]
    shape = smoothing.shape
    lane = lanes_of(shape)
    row = lax.broadcasted_iota(jnp.int32, shape, 0)
    counts = jnp.zeros(shape, jnp.int32)
    for cell in range(cells):
        counts = jnp.where(row == cell, count[cell], counts)
    mass_live = jnp.where(lane < counts, mass[...], 0.0)
    zeros = jnp.zeros(shape, jnp.float32)
    rows = (
        position[0], position[1], position[2], mass_live,
        SPEED * velocity[0], SPEED * velocity[1], SPEED * velocity[2], 2.0 * smoothing[...],
        (ADIABATIC - 1.0) * energy[...], density_old[...], counts.astype(jnp.float32), zeros,
        jnp.where(active[...] > 0, 1.0, 0.0),
        STEP_MAX * jnp.exp2(-time_bin[...].astype(jnp.float32)), zeros, zeros,
    )
    for field, values in enumerate(rows):
        own[:, field, :] = values
    per_peer, peers = export.shape
    for peer in range(peers):
        for entry in range(per_peer):
            cell = export[entry, peer]
            outgoing[peer, entry * ROWS : (entry + 1) * ROWS, :] = own[cell, 0:ROWS, :]
            start = per_peer * ROWS + entry * SENT
            outgoing[peer, start : start + SENT, :] = own[cell, ROWS : ROWS + SENT, :]
    for side, cell in enumerate((cells - 1, 0)):
        border[side] = own[cell, 0 : ROWS + SENT, :]


def own_rows(own, field):
    return own[:, ROWS + field, :]


def sort_kernel(own, actives, bundle, spreads, columns):
    cells = own.shape[0]
    shape = (cells, LANES)
    lane = lanes_of(shape)
    ones = own_rows(own, ACTIVE)
    is_active = ones > 0.5
    for cell in range(cells):
        actives[0, cell] = jnp.sum(ones[cell : cell + 1, :]).astype(jnp.int32)
    square = (LANES, LANES)
    upper = lax.broadcasted_iota(jnp.int32, square, 0) <= lanes_of(square)
    upper = jnp.where(upper, 1.0, 0.0).astype(jnp.bfloat16)
    seen = jnp.dot(ones.astype(jnp.bfloat16), upper, preferred_element_type=jnp.float32)
    seen = seen.astype(jnp.int32)
    chosen = lane_gather(seen, jnp.full(shape, LANES - 1, jnp.int32))
    others = lane + 1 - seen
    rank = jnp.where(is_active, seen - 1, chosen + others - 1)
    first_part = lane < chosen
    wanted = jnp.where(first_part, lane, lane - chosen)
    slot = jnp.zeros(shape, jnp.int32)
    step = LANES // 2
    while step:
        probe = slot + (step - 1)
        found = jnp.where(first_part, lane_gather(seen, probe), lane_gather(others, probe))
        slot = jnp.where(found <= wanted, slot + step, slot)
        step //= 2
    bundle[:, S_HEAT, :] = lane_gather(own_rows(own, HEAT), slot)
    bundle[:, S_RANK, :] = rank.astype(jnp.float32)
    bundle[:, S_CHOSEN, :] = chosen.astype(jnp.float32)
    for spare in range(S_CHOSEN + 1, S_LOW):
        bundle[:, spare, :] = jnp.zeros(shape, jnp.float32)
    place = lax.broadcasted_iota(jnp.int32, (ROWS, LANES), 0) <= Z
    for cell in range(cells):
        order = jnp.broadcast_to(slot[cell : cell + 1, :], (ROWS, LANES))
        tile = lane_gather(own[cell, 0:ROWS, :], order)
        bundle[cell, 0:ROWS, :] = tile
        target = lane < chosen[cell : cell + 1, :]
        low = jnp.min(jnp.where(target, tile, FAR_AWAY), axis=1, keepdims=True)
        high = jnp.max(jnp.where(target, tile, -FAR_AWAY), axis=1, keepdims=True)
        bundle[cell, S_LOW : S_LOW + ROWS, :] = jnp.where(place, low, -FAR_AWAY)
        bundle[cell, S_HIGH : S_HIGH + ROWS, :] = jnp.where(place, high, FAR_AWAY)
        bundle[cell, S_REACH : S_REACH + 1, :] = jnp.broadcast_to(high[WIDE : WIDE + 1, :], (1, LANES))
        columns[cell, :, 0:ROWS] = tile.T

    def one_cell(cell, carry):
        def one_pair(pair, carry):
            base = pl.multiple_of(pair * 2 * ROWS, 2 * ROWS)
            mine = columns[cell, pl.ds(base, 2 * ROWS), :]
            for which, field in enumerate(SPREAD):
                tiles = spread(mine, field).reshape(2, ROWS, LANES)
                spreads[cell, pl.ds(pair * 2, 2), which * ROWS : (which + 1) * ROWS, :] = tiles
            return carry

        return lax.fori_loop(0, (actives[0, cell] + 2 * ROWS - 1) // (2 * ROWS), one_pair, carry)

    lax.fori_loop(0, cells, one_cell, 0)


def source_tiles(own, incoming, border, per_peer):
    cells, peers = own.shape[0], incoming.shape[0]
    for cell in range(cells):
        yield (
            cell, lambda c=cell: own[c, 0:ROWS, :], lambda c=cell: own[c, ROWS : ROWS + SENT, :]
        )
    for peer in range(peers):
        for entry in range(per_peer):
            near, sent = entry * ROWS, per_peer * ROWS + entry * SENT
            yield (
                cells + peer * per_peer + entry,
                lambda p=peer, n=near: incoming[p, n : n + ROWS, :],
                lambda p=peer, n=sent: incoming[p, n : n + SENT, :],
            )
    for side in range(2):
        yield (
            cells + peers * per_peer + side,
            lambda b=side: border[b, 0:ROWS, :],
            lambda b=side: border[b, ROWS : ROWS + SENT, :],
        )


def fill_shifts(shifts):
    row = lax.broadcasted_iota(jnp.int32, (ROWS, LANES), 0)
    for code in range(shifts.shape[0]):
        first, second, third = code // 9 - 1.0, code // 3 % 3 - 1.0, code % 3 - 1.0
        shifts[code] = jnp.where(
            row == X, first, jnp.where(row == Y, second, jnp.where(row == Z, third, 0.0))
        )


def start_of(starts, cell, pair):
    per_line = LANES // PAIR_ROWS
    return starts[cell // per_line, (cell % per_line) * PAIR_ROWS + pair]


def fill_stream(stream, load, sources, starts, orders, cell):
    shape = (ROWS, LANES)
    lane = lanes_of(shape)
    pairs = sources.shape[1]
    moved = []
    for pair in range(pairs):
        order = jnp.broadcast_to(orders[pl.ds(cell * PAIR_ROWS + pair, 1), :], shape)
        moved.append(lane_gather(load(sources[cell, pair], pair), order))
    for pair in range(pairs):
        start = start_of(starts, cell, pair)
        block = start >> 7
        stream[block + 1] = moved[pair]
        pltpu.store(stream.at[block], moved[pair], mask=lane >= (start & (LANES - 1)))
    end = start_of(starts, cell, pairs)
    block = end >> 7
    stream[block] = jnp.where(lane < (end & (LANES - 1)), stream[block], 0.0)
    for extra in range(1, SPARE):
        stream[block + extra] = jnp.zeros(shape, jnp.float32)


def spread(values, field):
    return lane_gather(values, jnp.full(values.shape, field, jnp.int32))


def over_targets(active, one_chunk):
    groups = (active + ROWS - 1) // ROWS
    large = jnp.maximum(groups - 2, 0) // 4
    rest = groups - 4 * large
    large = jnp.where(rest == 4, large + 1, large)

    def large_chunk(chunk, carry):
        one_chunk(pl.multiple_of(chunk * 4 * ROWS, ROWS), 4)
        return carry

    lax.fori_loop(0, large, large_chunk, 0)
    for size in (1, 2, 3, 5):

        @pl.when(rest == size)
        def _(size=size):
            one_chunk(pl.multiple_of(large * 4 * ROWS, ROWS), size)


def density_kernel(
    per_peer, pair_source, pair_shift, export, actives,
    own, incoming, border, bundle, spreads,
    density, densities, outgoing, outgoing_border,
    table, shifts, sums, lines,
):
    fill_shifts(shifts)
    cells, peers = own.shape[0], incoming.shape[0]
    for place, near, _ in source_tiles(own, incoming, border, per_peer):
        table[place] = near()

    def one_cell(cell, carry):
        def one_chunk(base, groups):
            size = groups * ROWS
            at = pl.ds(base // ROWS, groups)
            *place, wide = [
                spreads[cell, at, which * ROWS : (which + 1) * ROWS, :].reshape(size, LANES)
                for which in range(len(SPREAD))
            ]
            smooth = 0.5 * wide

            total = jnp.zeros((size, LANES), jnp.float32)
            for pair in range(pair_source.shape[1]):
                source, code = pair_source[cell, pair], pair_shift[cell, pair]
                s = lambda field: table[source, field : field + 1, :]
                shift = lambda field: shifts[code, field : field + 1, :]
                apart = [place[c] - (s(c) + shift(c)) for c in range(3)]
                square = apart[0] * apart[0] + apart[1] * apart[1] + apart[2] * apart[2]
                radius = pl.reciprocal(lax.rsqrt(square), approx=True)
                outer = jnp.maximum(wide - radius, 0.0)
                inner = jnp.maximum(smooth - radius, 0.0)
                value = outer * outer * outer - 4.0 * (inner * inner * inner)
                total = total + s(MASS) * value
            sums[cell, pl.ds(base, size), 0:1] = jnp.sum(total, axis=1, keepdims=True)

        over_targets(actives[0, cell], one_chunk)
        return carry

    lax.fori_loop(0, cells, one_cell, 0)
    for cell in range(cells):
        lines[cell : cell + 1, :] = sums[cell].T[0:1, :]
    inverse = 2.0 / bundle[:, WIDE, :]
    inverse = inverse * inverse * inverse
    summed = lines[...] * (0.25 / math.pi) * (inverse * inverse)
    rank = bundle[:, S_RANK, :].astype(jnp.int32)
    density[...] = jnp.where(
        own_rows(own, ACTIVE) > 0.5, lane_gather(summed, rank), own_rows(own, DENS)
    )
    densities[0] = summed
    densities[1] = density[...]
    for peer in range(peers):
        for entry in range(per_peer):
            outgoing[peer, entry : entry + 1, :] = density[pl.ds(export[entry, peer], 1), :]
    outgoing_border[0:1, :] = density[cells - 1 : cells, :]
    outgoing_border[1:2, :] = density[0:1, :]


def stream_kernel(
    per_peer, pair_source, pair_shift, own, incoming, border, bundle, densities,
    near_streams, starts, orders, columns, last, traits,
    near_table, supports, shifts, squares, reaches, starts_row, sem,
):
    fill_shifts(shifts)
    cells, pairs = pair_source.shape
    tile_shape = (ROWS, LANES)
    row = lax.broadcasted_iota(jnp.int32, tile_shape, 0)
    lane = lanes_of(tile_shape).astype(jnp.float32)
    for place, near, sent in source_tiles(own, incoming, border, per_peer):
        tile, other = near(), sent()
        near_table[place] = tile
        wide, at = tile[WIDE : WIDE + 1, :], slice(place, place + 1)
        traits[0, at, :] = other[HEAT : HEAT + 1, :]
        traits[1, at, :] = wide
        supports[at, :] = jnp.where(lane[0:1, :] < other[LIVE : LIVE + 1, :], wide, -FAR_AWAY)

    def measure(cell, carry):
        low = bundle[cell, S_LOW : S_LOW + ROWS, :]
        high = bundle[cell, S_HIGH : S_HIGH + ROWS, :]
        for pair in range(pairs):
            source = pair_source[cell, pair]
            tile = near_table[source] + shifts[pair_shift[cell, pair]]
            away = jnp.maximum(jnp.maximum(low - tile, tile - high), 0.0)
            squares[cell, pair * ROWS : (pair + 1) * ROWS, :] = away * away
            place = pl.ds(cell * PAIR_ROWS + pair, 1)
            reaches[place, :] = supports[pl.ds(source, 1), :]
        return carry

    lax.fori_loop(0, cells, measure, 0, unroll=2)
    shape = (PAIR_ROWS, pairs * ROWS)
    adder = lax.broadcasted_iota(jnp.int32, shape, 0) == (lanes_of(shape) // ROWS)
    adder = jnp.where(adder, 1.0, 0.0).astype(jnp.bfloat16)
    pair_row = lax.broadcasted_iota(jnp.int32, (PAIR_ROWS, LANES), 0)
    flags = []
    for cell in range(cells):
        distance = jnp.dot(
            adder, squares[cell].astype(jnp.bfloat16), preferred_element_type=jnp.float32
        )
        support = reaches[cell * PAIR_ROWS : (cell + 1) * PAIR_ROWS, :]
        limit = jnp.maximum(support, bundle[cell, S_REACH : S_REACH + 1, :])
        keep = (distance < 1.005 * limit * limit) & (support > 0.0) & (pair_row < pairs)
        target = lane[0:1, :] < bundle[cell, S_CHOSEN : S_CHOSEN + 1, :]
        keep = keep | ((pair_row == pairs) & target)
        flags.append(jnp.where(keep, 1.0, 0.0))
    flags = jnp.concatenate(flags, axis=0).astype(jnp.bfloat16)
    rows = flags.shape[0]
    shape = (rows, rows)
    first, second = lax.broadcasted_iota(jnp.int32, shape, 0), lanes_of(shape)
    same = (first // PAIR_ROWS) == (second // PAIR_ROWS)
    earlier = jnp.where(same & (second < first), 1.0, 0.0).astype(jnp.bfloat16)
    later = jnp.where(same & (first < second), 1.0, 0.0).astype(jnp.bfloat16)
    dot = functools.partial(jnp.dot, preferred_element_type=jnp.float32)
    sums = lax.dot_general(
        jnp.ones((ROWS, LANES), jnp.bfloat16), flags, (((1,), (1,)), ((), ())),
        preferred_element_type=jnp.float32,
    )
    sums = dot(sums.astype(jnp.bfloat16), later)
    for line in range(starts_row.shape[0]):
        starts_row[line : line + 1, :] = sums[0:1, line * LANES : (line + 1) * LANES].astype(
            jnp.int32
        )
    copy = pltpu.make_async_copy(starts_row, starts, sem)
    copy.start()
    square = (LANES, LANES)
    upper = lax.broadcasted_iota(jnp.int32, square, 0) <= lanes_of(square)
    upper = jnp.where(upper, 1.0, 0.0).astype(jnp.bfloat16)
    seen = dot(flags, upper)
    begins = dot(earlier, dot(flags, jnp.ones(square, jnp.bfloat16)).astype(jnp.bfloat16))
    wanted = (lanes_of(seen.shape) - begins.astype(jnp.int32)) & (LANES - 1)
    wanted = wanted.astype(jnp.float32)
    slot = jnp.zeros(seen.shape, jnp.int32)
    step = LANES // 2
    while step:
        found = lane_gather(seen, slot + (step - 1))
        slot = jnp.where(found <= wanted, slot + step, slot)
        step //= 2
    orders[...] = slot
    heat, summed = bundle[:, S_HEAT, :], densities[0]
    fields = (jnp.sqrt(ADIABATIC * heat), 4.0 * summed)
    for cell in range(cells):
        tile = jnp.zeros(tile_shape, jnp.float32)
        for which, values in enumerate(fields):
            tile = jnp.where(row == which, values[cell : cell + 1, :], tile)
        columns[cell, :, 0 : 2 * ROWS] = jnp.concatenate([bundle[cell, 0:ROWS, :], tile], axis=0).T
    last[:, F_RANK, :] = bundle[:, S_RANK, :]
    last[:, F_ACTIVE, :] = own_rows(own, ACTIVE)
    last[:, F_STEP, :] = own_rows(own, STEP)
    for from_row, to_row in ((VX, F_VX), (VY, F_VY), (VZ, F_VZ)):
        last[:, to_row, :] = own[:, from_row, :] * (1.0 / SPEED)
    last[:, F_DENS, :] = densities[1]
    last[:, F_DENS + 1, :] = jnp.zeros((cells, LANES), jnp.float32)
    copy.wait()

    def one_cell(cell, carry):
        load = lambda source, pair: near_table[source] + shifts[pair_shift[cell, pair]]
        fill_stream(near_streams.at[cell], load, pair_source, starts, orders, cell)
        return carry

    lax.fori_loop(0, cells, one_cell, 0, unroll=2)


def force_kernel(
    per_peer, pair_source, starts,
    columns, orders, last, traits, new_density, new_border, near_streams,
    acceleration, kicked,
    table, densities, streams, sums, lines,
):
    cells, peers = last.shape[0], new_density.shape[0]
    pairs = pair_source.shape[1]
    for cell in range(cells):
        densities[cell : cell + 1, :] = last[cell, F_DENS : F_DENS + 1, :]
    for peer in range(peers):
        place = cells + peer * per_peer
        densities[place : place + per_peer, :] = new_density[peer]
    place = cells + peers * per_peer
    densities[place : place + 2, :] = new_border[...]
    heat, wide = traits[0], traits[1]
    inverse = 2.0 * pl.reciprocal(wide, approx=True)
    inverse = inverse * inverse * inverse
    table[:, DENS4, :] = 4.0 * densities[...]
    table[:, PRESS, :] = heat * pl.reciprocal(densities[...], approx=True)
    table[:, INV6, :] = inverse * inverse
    table[:, HALF, :] = 0.025 * wide
    table[:, SOUND, :] = jnp.sqrt(ADIABATIC * heat)

    def one_stream(cell, carry):
        fill_stream(
            streams.at[cell], lambda source, pair: table[source], pair_source, starts, orders, cell
        )
        return carry

    lax.fori_loop(0, cells, one_stream, 0, unroll=4)

    def one_cell(cell, carry):
        near, far = near_streams.at[cell], streams.at[cell]
        end = start_of(starts, cell, pairs)
        used = (end + LANES - 1) >> 7
        rounds = (used + FORCE_UNROLL - 1) // FORCE_UNROLL

        def one_chunk(base, groups):
            size = groups * ROWS
            mine = columns[cell, pl.ds(base, size), :]
            place = [spread(mine, field) for field in (X, Y, Z)]
            wide = spread(mine, WIDE)
            speed = [spread(mine, field) for field in (VX, VY, VZ)]
            sound, dens4 = [spread(mine, ROWS + field) for field in range(2)]
            inv6 = 2.0 * pl.reciprocal(wide, approx=True)
            inv6 = inv6 * inv6 * inv6
            inv6 = inv6 * inv6
            half_ = 0.025 * wide
            press = sound * sound * ((4.0 / ADIABATIC) * pl.reciprocal(dens4, approx=True))

            def blocks(index, totals):
                for sub in range(FORCE_UNROLL):
                    block = index * FORCE_UNROLL + sub
                    s = lambda field: near[block, field : field + 1, :]
                    o = lambda field: far[block, field : field + 1, :]
                    apart = [place[c] - s(c) for c in range(3)]
                    square = apart[0] * apart[0] + apart[1] * apart[1] + apart[2] * apart[2]
                    inverse = lax.rsqrt(jnp.maximum(square, 1e-24))
                    radius = pl.reciprocal(inverse, approx=True)
                    outer = jnp.maximum(wide - radius, 0.0)
                    least = jnp.minimum(outer, radius)
                    slope = inv6 * (least * ((outer + outer) - least))
                    outer = jnp.maximum(s(WIDE) - radius, 0.0)
                    least = jnp.minimum(outer, radius)
                    slope = slope + o(INV6) * (least * ((outer + outer) - least))
                    approach = (
                        (speed[0] - s(VX)) * apart[0]
                        + (speed[1] - s(VY)) * apart[1]
                        + (speed[2] - s(VZ)) * apart[2]
                    )
                    half = half_ + o(HALF)
                    slow = pl.reciprocal(square + half * half, approx=True)
                    mu = half * jnp.minimum(approach, 0.0) * slow
                    light = pl.reciprocal(dens4 + o(DENS4), approx=True)
                    viscous = mu * (mu - (sound + o(SOUND))) * light
                    weight = (press + o(PRESS) + viscous) * (slope * (inverse * s(MASS)))
                    terms = [weight * a for a in apart]
                    totals = terms if totals is None else [t + a for t, a in zip(totals, terms)]
                return tuple(totals)

            totals = lax.fori_loop(1, rounds, blocks, blocks(0, None))
            for c in range(3):
                sums[cell, pl.ds(base, size), c : c + 1] = jnp.sum(
                    totals[c], axis=1, keepdims=True
                )

        over_targets(start_of(starts, cell, pairs + 1) - end, one_chunk)
        return carry

    lax.fori_loop(0, cells, one_cell, 0)
    for cell in range(cells):
        turned = sums[cell].T
        for c in range(3):
            lines[c, cell : cell + 1, :] = turned[c : c + 1, :]
    rank = last[:, F_RANK, :].astype(jnp.int32)
    for c in range(3):
        gathered = lane_gather(lines[c] * (0.375 / math.pi), rank)
        value = jnp.where(last[:, F_ACTIVE, :] > 0.5, gathered, 0.0)
        acceleration[c] = value
        kicked[c] = last[:, F_VX + c, :] + value * last[:, F_STEP, :]


def shards(
    position, velocity, smoothing, particle_mass, energy, density_old, cell_count, active,
    time_bin, pair_source, pair_shift, export,
):
    cells, capacity = smoothing.shape
    peers, per_peer = export.shape
    sources = cells + peers * per_peer + 2
    codes = 27
    f32 = lambda *shape: jax.ShapeDtypeStruct(shape, jnp.float32)
    smem = pl.BlockSpec(memory_space=pltpu.SMEM)
    vmem = pl.BlockSpec(memory_space=pltpu.VMEM)
    hbm = pl.BlockSpec(memory_space=pltpu.HBM)
    whole = pltpu.CompilerParams(vmem_limit_bytes=64 * 2**20)
    params = pltpu.CompilerParams(vmem_limit_bytes=24 * 2**20)
    cost = pl.CostEstimate(flops=10**9, bytes_accessed=1000, transcendentals=0)
    i32 = lambda *shape: jax.ShapeDtypeStruct(shape, jnp.int32)
    sent_rows = per_peer * (ROWS + SENT)
    turned = export.T

    def landing(scalars, *arrays):
        return (
            [pltpu.SMEM(a.shape, a.dtype) for a in arrays[:scalars]]
            + [pltpu.VMEM(a.shape, a.dtype) for a in arrays[scalars:]]
            + [pltpu.SemaphoreType.DMA((len(arrays),))]
        )

    arrays = (
        cell_count, turned, position, velocity, smoothing, particle_mass, energy, density_old,
        active, time_bin,
    )
    own, outgoing, border = pl.pallas_call(
        pack_kernel,
        out_shape=(
            f32(cells, 2 * ROWS, capacity),
            f32(peers, sent_rows, capacity),
            f32(2, ROWS + SENT, capacity),
        ),
        in_specs=[hbm] * 10,
        out_specs=(vmem,) * 3,
        scratch_shapes=landing(2, *arrays),
        compiler_params=whole,
        cost_estimate=cost,
        name="pack",
    )(*arrays)

    def exchange(pieces):
        return lax.all_to_all(pieces, "cell", split_axis=0, concat_axis=0, tiled=True)

    def swap_border(pieces):
        size = lax.axis_size("region")
        up = [(i, (i + 1) % size) for i in range(size)]
        down = [(j, i) for i, j in up]
        if size == 2:
            return lax.ppermute(pieces, "region", up)
        before = lax.ppermute(pieces[0:1], "region", up)
        after = lax.ppermute(pieces[1:2], "region", down)
        return jnp.concatenate([before, after], axis=0)

    incoming = exchange(outgoing)
    other = swap_border(border)
    actives, bundle, spreads = pl.pallas_call(
        sort_kernel,
        out_shape=(
            i32(1, cells),
            f32(cells, S_ROWS, capacity),
            f32(cells, capacity // ROWS, len(SPREAD) * ROWS, capacity),
        ),
        in_specs=[vmem],
        out_specs=(smem, vmem, vmem),
        scratch_shapes=[pltpu.VMEM((cells, capacity, LANES), jnp.float32)],
        compiler_params=params,
        cost_estimate=cost,
        name="sort",
    )(own)

    density, densities, outgoing_density, border_density = pl.pallas_call(
        functools.partial(density_kernel, per_peer),
        out_shape=(
            f32(cells, capacity),
            f32(2, cells, capacity),
            f32(peers, per_peer, capacity),
            f32(2, capacity),
        ),
        in_specs=[smem] * 4 + [vmem] * 5,
        out_specs=(vmem,) * 4,
        scratch_shapes=[
            pltpu.VMEM((sources, ROWS, capacity), jnp.float32),
            pltpu.VMEM((codes, ROWS, capacity), jnp.float32),
            pltpu.VMEM((cells, capacity, ROWS), jnp.float32),
            pltpu.VMEM((cells, capacity), jnp.float32),
        ],
        compiler_params=params,
        cost_estimate=cost,
        name="density",
    )(pair_source, pair_shift, turned, actives, own, incoming, other, bundle, spreads)

    new_density = exchange(outgoing_density)
    new_border = swap_border(border_density)
    pairs = pair_source.shape[1]
    blocks = pairs + SPARE
    pair_rows = cells * PAIR_ROWS
    source_rows = -(-sources // ROWS) * ROWS
    near_streams, starts, orders, columns, last, traits = pl.pallas_call(
        functools.partial(stream_kernel, per_peer),
        out_shape=(
            f32(cells, blocks, ROWS, capacity),
            i32(pair_rows // capacity, capacity),
            i32(pair_rows, capacity),
            f32(cells, capacity, LANES),
            f32(cells, ROWS, capacity),
            f32(2, source_rows, capacity),
        ),
        in_specs=[smem] * 2 + [vmem] * 5,
        out_specs=(vmem, smem, vmem, vmem, vmem, vmem),
        scratch_shapes=[
            pltpu.VMEM((sources, ROWS, capacity), jnp.float32),
            pltpu.VMEM((source_rows, capacity), jnp.float32),
            pltpu.VMEM((codes, ROWS, capacity), jnp.float32),
            pltpu.VMEM((cells, pairs * ROWS, capacity), jnp.float32),
            pltpu.VMEM((pair_rows, capacity), jnp.float32),
            pltpu.VMEM((pair_rows // capacity, capacity), jnp.int32),
            pltpu.SemaphoreType.DMA,
        ],
        compiler_params=params,
        cost_estimate=cost,
        name="streams",
    )(pair_source, pair_shift, own, incoming, other, bundle, densities)

    acceleration, kicked = pl.pallas_call(
        functools.partial(force_kernel, per_peer),
        out_shape=(f32(3, cells, capacity), f32(3, cells, capacity)),
        in_specs=[smem] * 2 + [vmem] * 7,
        out_specs=(vmem,) * 2,
        scratch_shapes=[
            pltpu.VMEM((source_rows, ROWS, capacity), jnp.float32),
            pltpu.VMEM((source_rows, capacity), jnp.float32),
            pltpu.VMEM((cells, blocks, ROWS, capacity), jnp.float32),
            pltpu.VMEM((cells, capacity, ROWS), jnp.float32),
            pltpu.VMEM((3, cells, capacity), jnp.float32),
        ],
        compiler_params=params,
        cost_estimate=cost,
        name="force",
    )(
        pair_source, starts, columns, orders, last, traits, new_density, new_border, near_streams,
    )
    return density, acceleration, kicked


def solution(mesh):
    rows = P(("region", "cell"), None)
    planes = P(None, ("region", "cell"), None)
    return jax.shard_map(
        shards,
        mesh=mesh,
        in_specs=(
            planes, planes, rows, rows, rows, rows, P(("region", "cell")), rows, rows, rows, rows,
            rows,
        ),
        out_specs=(rows, planes, planes),
        check_vma=False,
    )
```

profile of v0, /device:TPU:0, one launch (start us, length us, event | category | flops | bytes accessed | tf_op | source)
XLA Modules:
  0.0 40.4 jit_solution(9523080383174488640)
XLA Ops:
  0.6 1.6 %pack.1 = (f32[8,16,128]{2,1,0:T(8,128)}, f32[16,24,128]{2,1,0:T(8,128)}, f32[2,12,128]{2,1,0:T(8,128)}) custom-call(s32[8]{0:T(128)} %refs_0_.1, s32[2,16]{1,0:T(2,128)} %bitcast.1, f32[3,8,128]{2,1,0:T(8,128)} %refs_2_.1, f32[3,8,128]{2,1,0:T(8,128)} %refs_3_.1, f32[8,128]{1,0:T(8,128)} %refs_4_.1, f32[8,128]{1,0:T(8,128)} %refs_5_.1, f32[8,128]{1,0:T(8,128)} %refs_6_.1, ...), custom_call_target="tpu_custom_call" | custom-call | flops 1000000000 | bytes 1000 | tf_op jit(solution)/shard_map/pack/pallas_call | solution.py:517
  2.3 0.0 copy-start
  2.3 0.0 copy-start.1
  2.3 0.0 copy-start.2
  2.3 0.0 copy-start.4
  2.3 7.5 %all-to-all-start = ((f32[16,24,128]{2,1,0:T(8,128)}), f32[16,24,128]{2,1,0:T(8,128)S(1)}, u32[]{:S(2)}, u32[]{:S(2)}) async-start(f32[16,24,128]{2,1,0:T(8,128)} %get-tuple-element.23), calls=%async_computation | async-start | bytes 393216 | tf_op jit(solution)/shard_map/all_to_all | solution.py:533
  9.8 1.6 %collective-permute-start = (f32[2,12,128]{2,1,0:T(8,128)}, f32[2,12,128]{2,1,0:T(8,128)S(1)}, u32[]{:S(2)}, u32[]{:S(2)}) collective-permute-start(f32[2,12,128]{2,1,0:T(8,128)} %get-tuple-element.24), channel_id=1, source_target_pairs={{0,16},{16,0},{1,17},{17,1},{2,18},{18,2},{3,19},{19,3},{4,20},{20... | collective-permute-start | bytes 36872 | tf_op jit(solution)/shard_map/ppermute | solution.py:540
  11.4 0.0 copy-start.3
  11.4 0.8 %copy-done.3 = f32[8,16,128]{2,1,0:T(8,128)S(1)} copy-done((f32[8,16,128]{2,1,0:T(8,128)S(1)}, f32[8,16,128]{2,1,0:T(8,128)}, u32[]{:S(2)}) %copy-start.3) | copy-done | bytes 65560
  12.3 2.8 %sort.1 = (s32[1,8]{1,0:T(1,128)S(1)}, f32[8,32,128]{2,1,0:T(8,128)S(1)}, f32[8,16,32,128]{3,2,1,0:T(8,128)S(1)}) custom-call(f32[8,16,128]{2,1,0:T(8,128)S(1)} %copy-done.3), custom_call_target="tpu_custom_call" | custom-call | flops 1000000000 | bytes 1000 | tf_op jit(solution)/shard_map/sort/pallas_call | solution.py:547
  15.1 0.0 collective-permute-done.border
  15.1 3.7 %all-to-all-done.incoming = f32[16,24,128]{2,1,0:T(8,128)S(1)} async-done(((f32[16,24,128]{2,1,0:T(8,128)}), f32[16,24,128]{2,1,0:T(8,128)S(1)}, u32[]{:S(2)}, u32[]{:S(2)}) %all-to-all-start) | async-done | bytes 196640 | tf_op jit(solution)/shard_map/all_to_all | solution.py:533
  18.8 0.0 copy-done
  18.8 0.0 copy-done.1
  18.8 0.0 copy-done.2
  18.8 0.0 copy-done.4
  18.9 4.6 %density.1 = (f32[8,128]{1,0:T(8,128)}, f32[2,8,128]{2,1,0:T(8,128)S(1)}, f32[16,2,128]{2,1,0:T(2,128)}, f32[2,128]{1,0:T(2,128)S(1)}) custom-call(s32[8,27]{1,0:T(8,128)S(1)} %copy-done.1, s32[8,27]{1,0:T(8,128)S(1)} %copy-done, s32[2,16]{1,0:T(2,128)S(1)} %bitcast.2, s32[1,8]{1,0:T(1,128)S(1)} %get-tuple-element.22.actives, f32[8,16,128]{2,1,0:T(8,128)S(1)} %copy-done.4, ...), custom_call_target="tpu_custom_call" | custom-call | flops 1000000000 | bytes 1000 | tf_op jit(solution)/shard_map/density/pallas_call | solution.py:562
  23.5 3.5 %all-to-all-start.1 = ((f32[16,2,128]{2,1,0:T(2,128)}), f32[16,2,128]{2,1,0:T(2,128)S(1)}, u32[]{:S(2)}, u32[]{:S(2)}) async-start(f32[16,2,128]{2,1,0:T(2,128)} %get-tuple-element.34), calls=%async_computation.1 | async-start | bytes 32768 | tf_op jit(solution)/shard_map/all_to_all | solution.py:533
  27.0 0.6 %collective-permute-start.1 = (f32[2,128]{1,0:T(2,128)S(1)}, f32[2,128]{1,0:T(2,128)S(1)}, u32[]{:S(2)}, u32[]{:S(2)}) collective-permute-start(f32[2,128]{1,0:T(2,128)S(1)} %get-tuple-element.35), channel_id=1, source_target_pairs={{0,16},{16,0},{1,17},{17,1},{2,18},{18,2},{3,19},{19,3},{4,20},{20... | collective-permute-start | bytes 3080 | tf_op jit(solution)/shard_map/ppermute | solution.py:540
  27.6 4.5 %streams.1 = (f32[8,34,8,128]{3,2,1,0:T(8,128)S(1)}, s32[2,128]{1,0:T(2,128)S(1)}, s32[256,128]{1,0:T(8,128)S(1)}, f32[8,128,128]{2,1,0:T(8,128)S(1)}, f32[8,8,1...) custom-call(s32[8,27]{1,0:T(8,128)S(1)} %copy-done.1, s32[8,27]{1,0:T(8,128)S(1)} %copy-done, f32[8,16,128]{2,1,0:T(8,128)S(1)} %copy-done.4, ...), custom_call_target="tpu_custom_call" | custom-call | flops 1000000000 | bytes 1000 | tf_op jit(solution)/shard_map/streams/pallas_call | solution.py:589
  32.1 0.0 collective-permute-done.1.new_border
  32.1 1.3 %all-to-all-done.1.new_density = f32[16,2,128]{2,1,0:T(2,128)S(1)} async-done(((f32[16,2,128]{2,1,0:T(2,128)}), f32[16,2,128]{2,1,0:T(2,128)S(1)}, u32[]{:S(2)}, u32[]{:S(2)}) %all-to-all-start.1) | async-done | bytes 16416 | tf_op jit(solution)/shard_map/all_to_all | solution.py:533
  33.4 6.9 %force.1 = (f32[3,8,128]{2,1,0:T(8,128)}, f32[3,8,128]{2,1,0:T(8,128)}) custom-call(s32[8,27]{1,0:T(8,128)S(1)} %copy-done.1, s32[2,128]{1,0:T(2,128)S(1)} %get-tuple-element.29.starts, f32[8,128,128]{2,1,0:T(8,128)S(1)} %get-tuple-element.30.columns, s32[256,128]{1,0:T(8,128)S(1)} %get-tuple-element.31.orders, f32[8,8,128]{2,1,0:T(8,128)S(1)} %get-tuple-element.32.last, ...), custom_call_target="tpu_custom_call" | custom-call | flops 1000000000 | bytes 1000 | tf_op jit(solution)/shard_map/force/pallas_call | solution.py:615
Async XLA Ops:
  2.3 16.6 %copy-start = (s32[8,27]{1,0:T(8,128)S(1)}, s32[8,27]{1,0:T(8,128)}, u32[]{:S(2)}) copy-start(s32[8,27]{1,0:T(8,128)} %pair_shift.3) | copy-start | bytes 2596
  2.3 16.5 %copy-start.1 = (s32[8,27]{1,0:T(8,128)S(1)}, s32[8,27]{1,0:T(8,128)}, u32[]{:S(2)}) copy-start(s32[8,27]{1,0:T(8,128)} %pair_source.5) | copy-start | bytes 2596
  2.3 16.5 %copy-start.2 = (s32[16,2]{0,1:T(2,128)S(1)}, s32[16,2]{0,1:T(2,128)}, u32[]{:S(2)}) copy-start(s32[16,2]{0,1:T(2,128)} %param.23) | copy-start | bytes 388
  2.3 16.5 %copy-start.4 = (f32[8,16,128]{2,1,0:T(8,128)S(1)}, f32[8,16,128]{2,1,0:T(8,128)}, u32[]{:S(2)}) copy-start(f32[8,16,128]{2,1,0:T(8,128)} %get-tuple-element.21.own) | copy-start | bytes 196612
  2.3 16.5 %all-to-all-start = ((f32[16,24,128]{2,1,0:T(8,128)}), f32[16,24,128]{2,1,0:T(8,128)S(1)}, u32[]{:S(2)}, u32[]{:S(2)}) async-start(f32[16,24,128]{2,1,0:T(8,128)} %get-tuple-element.23), calls=%async_computation | async-start | bytes 393216 | tf_op jit(solution)/shard_map/all_to_all | solution.py:533
  9.8 5.2 %collective-permute-start = (f32[2,12,128]{2,1,0:T(8,128)}, f32[2,12,128]{2,1,0:T(8,128)S(1)}, u32[]{:S(2)}, u32[]{:S(2)}) collective-permute-start(f32[2,12,128]{2,1,0:T(8,128)} %get-tuple-element.24), channel_id=1, source_target_pairs={{0,16},{16,0},{1,17},{17,1},{2,18},{18,2},{3,19},{19,3},{4,20},{20... | collective-permute-start | bytes 36872 | tf_op jit(solution)/shard_map/ppermute | solution.py:540
  11.4 0.8 %copy-start.3 = (f32[8,16,128]{2,1,0:T(8,128)S(1)}, f32[8,16,128]{2,1,0:T(8,128)}, u32[]{:S(2)}) copy-start(f32[8,16,128]{2,1,0:T(8,128)} %get-tuple-element.21.own) | copy-start | bytes 196612
  23.5 9.9 %all-to-all-start.1 = ((f32[16,2,128]{2,1,0:T(2,128)}), f32[16,2,128]{2,1,0:T(2,128)S(1)}, u32[]{:S(2)}, u32[]{:S(2)}) async-start(f32[16,2,128]{2,1,0:T(2,128)} %get-tuple-element.34), calls=%async_computation.1 | async-start | bytes 32768 | tf_op jit(solution)/shard_map/all_to_all | solution.py:533
  27.0 5.1 %collective-permute-start.1 = (f32[2,128]{1,0:T(2,128)S(1)}, f32[2,128]{1,0:T(2,128)S(1)}, u32[]{:S(2)}, u32[]{:S(2)}) collective-permute-start(f32[2,128]{1,0:T(2,128)S(1)} %get-tuple-element.35), channel_id=1, source_target_pairs={{0,16},{16,0},{1,17},{17,1},{2,18},{18,2},{3,19},{19,3},{4,20},{20... | collective-permute-start | bytes 3080 | tf_op jit(solution)/shard_map/ppermute | solution.py:540
where the time goes:
time: 40.8 us; the launch traced here: 40.4 us
  Pallas kernels  20.5 us (50%)
  starting transfers between devices  13.2 us (32%)
  waiting for transfers between devices  5.09 us (12%)
  local copies, waits for them, and re-layouts  0.86 us (2%)
  between operations  0.74 us (2%)
    all_to_all x2, starting transfers between devices, exchange(): lax.all_to_all(pieces, 'cell', split_axis=0, concat_axis=0, tiled=True)  11 us
    pallas_call x1, Pallas kernels, shards(): pl.pallas_call(functools.partial(force_kernel, per_peer), out_shape=(f32(...  6.93 us
    all_to_all x2, waiting for transfers between devices, exchange(): lax.all_to_all(pieces, 'cell', split_axis=0, concat_axis=0, tiled=True)  5.09 us
    pallas_call x1, Pallas kernels, shards(): pl.pallas_call(functools.partial(density_kernel, per_peer), out_shape=(f3...  4.62 us
    pallas_call x1, Pallas kernels, shards(): pl.pallas_call(functools.partial(stream_kernel, per_peer), out_shape=(f32...  4.47 us
    pallas_call x1, Pallas kernels, shards(): pl.pallas_call(sort_kernel, out_shape=(i32(1, cells), f32(cells, S_ROWS,...  2.81 us
    ppermute x2, starting transfers between devices, swap_border(): return lax.ppermute(pieces, 'region', up)  2.21 us
    pallas_call x1, Pallas kernels, shards(): pl.pallas_call(pack_kernel, out_shape=(f32(cells, 2 * ROWS, capacity), f3...  1.64 us
  transfers between devices with their start and end apart: 4, of which 2 were waited for; matrix products, arithmetic and copies ran while one was open for 0% of the time, Pallas kernels for 18%

commit v1 on v0

--- a/solution.py
+++ b/solution.py
@@ -308,7 +308,7 @@
             reaches[place, :] = supports[pl.ds(source, 1), :]
         return carry
 
-    lax.fori_loop(0, cells, measure, 0, unroll=2)
+    lax.fori_loop(0, cells, measure, 0, unroll=4)
     shape = (PAIR_ROWS, pairs * ROWS)
     adder = lax.broadcasted_iota(jnp.int32, shape, 0) == (lanes_of(shape) // ROWS)
     adder = jnp.where(adder, 1.0, 0.0).astype(jnp.bfloat16)
@@ -378,12 +378,12 @@
         fill_stream(near_streams.at[cell], load, pair_source, starts, orders, cell)
         return carry
 
-    lax.fori_loop(0, cells, one_cell, 0, unroll=2)
+    lax.fori_loop(0, cells, one_cell, 0, unroll=4)
 
 
 def force_kernel(
     per_peer, pair_source, starts,
-    columns, orders, last, traits, new_density, new_border, near_streams,
+    columns, orders, last, traits, new_density, new_border, near_streams, spreads,
     acceleration, kicked,
     table, densities, streams, sums, lines,
 ):
@@ -411,7 +411,7 @@
         )
         return carry
 
-    lax.fori_loop(0, cells, one_stream, 0, unroll=4)
+    lax.fori_loop(0, cells, one_stream, 0, unroll=8)
 
     def one_cell(cell, carry):
         near, far = near_streams.at[cell], streams.at[cell]
@@ -422,8 +422,11 @@
         def one_chunk(base, groups):
             size = groups * ROWS
             mine = columns[cell, pl.ds(base, size), :]
-            place = [spread(mine, field) for field in (X, Y, Z)]
-            wide = spread(mine, WIDE)
+            at = pl.ds(base // ROWS, groups)
+            *place, wide = [
+                spreads[cell, at, which * ROWS : (which + 1) * ROWS, :].reshape(size, LANES)
+                for which in range(len(SPREAD))
+            ]
             speed = [spread(mine, field) for field in (VX, VY, VZ)]
             sound, dens4 = [spread(mine, ROWS + field) for field in range(2)]
             inv6 = 2.0 * pl.reciprocal(wide, approx=True)
@@ -615,7 +618,7 @@
     acceleration, kicked = pl.pallas_call(
         functools.partial(force_kernel, per_peer),
         out_shape=(f32(3, cells, capacity), f32(3, cells, capacity)),
-        in_specs=[smem] * 2 + [vmem] * 7,
+        in_specs=[smem] * 2 + [vmem] * 8,
         out_specs=(vmem,) * 2,
         scratch_shapes=[
             pltpu.VMEM((source_rows, ROWS, capacity), jnp.float32),
@@ -629,6 +632,7 @@
         name="force",
     )(
         pair_source, starts, columns, orders, last, traits, new_density, new_border, near_streams,
+        spreads,
     )
     return density, acceleration, kicked
 

time: 40.8 us -> 53.3 us (1.31)
  the two profiles are of different devices: /device:TPU:0 before, /device:TPU:26 now
where the time goes in v1:
time: 53.3 us; the launch traced here: 52.8 us
  Pallas kernels  24.1 us (45%)
  starting transfers between devices  14.1 us (26%)
  local copies, waits for them, and re-layouts  13.8 us (26%)
  between operations  0.78 us (1%)
    unnamed x50, local copies, waits for them, and re-layouts  13.8 us
    all_to_all x2, starting transfers between devices, exchange(): lax.all_to_all(pieces, 'cell', split_axis=0, concat_axis=0, tiled=True)  12.2 us
    pallas_call x1, Pallas kernels, shards(): pl.pallas_call(functools.partial(force_kernel, per_peer), out_shape=(f32(...  9.13 us
    pallas_call x1, Pallas kernels, shards(): pl.pallas_call(functools.partial(density_kernel, per_peer), out_shape=(f3...  5.54 us
    pallas_call x1, Pallas kernels, shards(): pl.pallas_call(functools.partial(stream_kernel, per_peer), out_shape=(f32...  4.51 us
    pallas_call x1, Pallas kernels, shards(): pl.pallas_call(sort_kernel, out_shape=(i32(1, cells), f32(cells, S_ROWS,...  3.27 us
    ppermute x2, starting transfers between devices, swap_border(): return lax.ppermute(pieces, 'region', up)  1.94 us
    pallas_call x1, Pallas kernels, shards(): pl.pallas_call(pack_kernel, out_shape=(f32(cells, 2 * ROWS, capacity), f3...  1.64 us
  transfers between devices with their start and end apart: 4, of which 0 were waited for; matrix products, arithmetic and copies ran while one was open for 0% of the time, Pallas kernels for 15%

profile of v1, /device:TPU:26, one launch (start us, length us, event | category | flops | bytes accessed | tf_op | source)
XLA Modules:
  0.0 52.8 jit_solution(13196485804603589771)
XLA Ops:
  0.6 1.6 %pack.1 = (f32[8,16,128]{2,1,0:T(8,128)}, f32[16,24,128]{2,1,0:T(8,128)}, f32[2,12,128]{2,1,0:T(8,128)}) custom-call(s32[8]{0:T(128)} %refs_0_.1, s32[2,16]{1,0:T(2,128)} %bitcast.1, f32[3,8,128]{2,1,0:T(8,128)} %refs_2_.1, f32[3,8,128]{2,1,0:T(8,128)} %refs_3_.1, f32[8,128]{1,0:T(8,128)} %refs_4_.1, f32[8,128]{1,0:T(8,128)} %refs_5_.1, f32[8,128]{1,0:T(8,128)} %refs_6_.1, ...), custom_call_target="tpu_custom_call" | custom-call | flops 1000000000 | bytes 1000 | tf_op jit(solution)/shard_map/pack/pallas_call | solution.py:520
  2.3 0.0 copy-start.6
  2.3 0.0 copy-start.15
  2.3 0.0 copy-start.17
  2.3 0.0 copy-start.21
  2.3 6.2 %all-to-all-start = ((f32[16,24,128]{2,1,0:T(8,128)}), f32[16,24,128]{2,1,0:T(8,128)S(1)}, u32[]{:S(2)}, u32[]{:S(2)}) async-start(f32[16,24,128]{2,1,0:T(8,128)} %get-tuple-element.23), calls=%async_computation | async-start | bytes 393216 | tf_op jit(solution)/shard_map/all_to_all | solution.py:536
  8.5 1.5 %collective-permute-start = (f32[2,12,128]{2,1,0:T(8,128)}, f32[2,12,128]{2,1,0:T(8,128)S(1)}, u32[]{:S(2)}, u32[]{:S(2)}) collective-permute-start(f32[2,12,128]{2,1,0:T(8,128)} %get-tuple-element.24), channel_id=1, source_target_pairs={{0,16},{16,0},{1,17},{17,1},{2,18},{18,2},{3,19},{19,3},{4,20},{20... | collective-permute-start | bytes 36872 | tf_op jit(solution)/shard_map/ppermute | solution.py:543
  10.0 0.8 %copy-done.20 = f32[8,16,128]{2,1,0:T(8,128)S(1)} copy-done((f32[8,16,128]{2,1,0:T(8,128)S(1)}, f32[8,16,128]{2,1,0:T(8,128)}, u32[]{:S(2)}) %copy-start.20) | copy-done | bytes 65560
  10.8 3.3 %sort.1 = (s32[1,8]{1,0:T(1,128)S(1)}, f32[8,32,128]{2,1,0:T(8,128)S(1)}, f32[8,16,32,128]{3,2,1,0:T(8,128)S(1)}) custom-call(f32[8,16,128]{2,1,0:T(8,128)S(1)} %copy-done.20), custom_call_target="tpu_custom_call" | custom-call | flops 1000000000 | bytes 1000 | tf_op jit(solution)/shard_map/sort/pallas_call | solution.py:550
  14.1 0.0 copy-start.18
  14.1 0.0 collective-permute-done.border
  14.1 0.0 copy-start.13
  14.2 0.0 all-to-all-done.incoming
  14.2 0.0 copy-done.6
  14.2 0.0 copy-done.15
  14.2 0.0 copy-done.17
  14.2 0.0 copy-done.21
  14.2 5.5 %density.1 = (f32[8,128]{1,0:T(8,128)}, f32[2,8,128]{2,1,0:T(8,128)S(1)}, f32[16,2,128]{2,1,0:T(2,128)}, f32[2,128]{1,0:T(2,128)}) custom-call(s32[8,27]{1,0:T(8,128)S(1)} %copy-done.6, s32[8,27]{1,0:T(8,128)S(1)} %copy-done.15, s32[2,16]{1,0:T(2,128)S(1)} %bitcast.2, s32[1,8]{1,0:T(1,128)S(1)} %get-tuple-element.22.actives, f32[8,16,128]{2,1,0:T(8,128)S(1)} %copy-done.21, ...), custom_call_target="tpu_custom_call" | custom-call | flops 1000000000 | bytes 1000 | tf_op jit(solution)/shard_map/density/pallas_call | solution.py:565
  19.7 0.0 copy-start.23
  19.8 0.6 %copy-done.23 = f32[2,8,128]{2,1,0:T(8,128)} copy-done((f32[2,8,128]{2,1,0:T(8,128)}, f32[2,8,128]{2,1,0:T(8,128)S(1)}, u32[]{:S(2)}) %copy-start.23) | copy-done | bytes 8216
  20.3 6.0 %all-to-all-start.1 = ((f32[16,2,128]{2,1,0:T(2,128)}), f32[16,2,128]{2,1,0:T(2,128)S(1)}, u32[]{:S(2)}, u32[]{:S(2)}) async-start(f32[16,2,128]{2,1,0:T(2,128)} %get-tuple-element.34), calls=%async_computation.1 | async-start | bytes 32768 | tf_op jit(solution)/shard_map/all_to_all | solution.py:536
  26.4 0.4 collective-permute-start.1
  26.8 0.0 copy-done.18
  26.8 0.0 copy-done.13
  26.8 0.0 copy-start.7
  26.8 0.7 %copy-done.7 = s32[8,27]{1,0:T(8,128)S(1)} copy-done((s32[8,27]{1,0:T(8,128)S(1)}, s32[8,27]{1,0:T(8,128)}, u32[]{:S(2)}) %copy-start.7) | copy-done | bytes 888
  27.5 0.0 copy-start.14
  27.5 0.7 %copy-done.14 = f32[2,12,128]{2,1,0:T(8,128)S(1)} copy-done((f32[2,12,128]{2,1,0:T(8,128)S(1)}, f32[2,12,128]{2,1,0:T(8,128)}, u32[]{:S(2)}) %copy-start.14) | copy-done | bytes 12312
  28.2 0.7 %copy-done.16 = s32[8,27]{1,0:T(8,128)S(1)} copy-done((s32[8,27]{1,0:T(8,128)S(1)}, s32[8,27]{1,0:T(8,128)}, u32[]{:S(2)}) %copy-start.16) | copy-done | bytes 888
  28.9 0.9 %copy-done.19 = f32[8,32,128]{2,1,0:T(8,128)S(1)} copy-done((f32[8,32,128]{2,1,0:T(8,128)S(1)}, f32[8,32,128]{2,1,0:T(8,128)}, u32[]{:S(2)}) %copy-start.19) | copy-done | bytes 131096
  29.8 0.8 %copy-done.22 = f32[8,16,128]{2,1,0:T(8,128)S(1)} copy-done((f32[8,16,128]{2,1,0:T(8,128)S(1)}, f32[8,16,128]{2,1,0:T(8,128)}, u32[]{:S(2)}) %copy-start.22) | copy-done | bytes 65560
  30.6 0.7 %copy-done.24 = f32[2,8,128]{2,1,0:T(8,128)S(1)} copy-done((f32[2,8,128]{2,1,0:T(8,128)S(1)}, f32[2,8,128]{2,1,0:T(8,128)}, u32[]{:S(2)}) %copy-start.24) | copy-done | bytes 8216
  31.3 4.5 %streams.1 = (f32[8,34,8,128]{3,2,1,0:T(8,128)S(1)}, s32[2,128]{1,0:T(2,128)S(1)}, s32[256,128]{1,0:T(8,128)S(1)}, f32[8,128,128]{2,1,0:T(8,128)S(1)}, f32[8,8,1...) custom-call(s32[8,27]{1,0:T(8,128)S(1)} %copy-done.7, s32[8,27]{1,0:T(8,128)S(1)} %copy-done.16, f32[8,16,128]{2,1,0:T(8,128)S(1)} %copy-done.22, ...), custom_call_target="tpu_custom_call" | custom-call | flops 1000000000 | bytes 1000 | tf_op jit(solution)/shard_map/streams/pallas_call | solution.py:592
  35.8 0.0 copy-start
  35.9 0.8 %copy-done = f32[8,128,128]{2,1,0:T(8,128)} copy-done((f32[8,128,128]{2,1,0:T(8,128)}, f32[8,128,128]{2,1,0:T(8,128)S(1)}, u32[]{:S(2)}) %copy-start) | copy-done | bytes 524312
  36.6 0.6 %copy-done.2 = f32[2,48,128]{2,1,0:T(8,128)} copy-done((f32[2,48,128]{2,1,0:T(8,128)}, f32[2,48,128]{2,1,0:T(8,128)S(1)}, u32[]{:S(2)}) %copy-start.2) | copy-done | bytes 49176
  37.2 0.6 %copy-done.4 = f32[8,8,128]{2,1,0:T(8,128)} copy-done((f32[8,8,128]{2,1,0:T(8,128)}, f32[8,8,128]{2,1,0:T(8,128)S(1)}, u32[]{:S(2)}) %copy-start.4) | copy-done | bytes 32792
  37.9 0.6 %copy-done.11 = s32[2,128]{1,0:T(2,128)} copy-done((s32[2,128]{1,0:T(2,128)}, s32[2,128]{1,0:T(2,128)S(1)}, u32[]{:S(2)}) %copy-start.11) | copy-done | bytes 1048
  38.4 0.0 collective-permute-done.1.new_border
  38.4 0.6 %copy-done.9 = f32[2,128]{1,0:T(2,128)} copy-done((f32[2,128]{1,0:T(2,128)}, f32[2,128]{1,0:T(2,128)S(1)}, u32[]{:S(2)}) %copy-start.9) | copy-done | bytes 1048
  39.0 0.0 all-to-all-done.1.new_density
  39.0 1.0 %copy-done.1 = f32[8,128,128]{2,1,0:T(8,128)S(1)} copy-done((f32[8,128,128]{2,1,0:T(8,128)S(1)}, f32[8,128,128]{2,1,0:T(8,128)}, u32[]{:S(2)}) %copy-start.1) | copy-done | bytes 524312
  40.0 0.8 %copy-done.3 = f32[2,48,128]{2,1,0:T(8,128)S(1)} copy-done((f32[2,48,128]{2,1,0:T(8,128)S(1)}, f32[2,48,128]{2,1,0:T(8,128)}, u32[]{:S(2)}) %copy-start.3) | copy-done | bytes 49176
  40.8 0.8 %copy-done.5 = f32[8,8,128]{2,1,0:T(8,128)S(1)} copy-done((f32[8,8,128]{2,1,0:T(8,128)S(1)}, f32[8,8,128]{2,1,0:T(8,128)}, u32[]{:S(2)}) %copy-start.5) | copy-done | bytes 32792
  41.6 0.7 %copy-done.8 = s32[8,27]{1,0:T(8,128)S(1)} copy-done((s32[8,27]{1,0:T(8,128)S(1)}, s32[8,27]{1,0:T(8,128)}, u32[]{:S(2)}) %copy-start.8) | copy-done | bytes 888
  42.3 0.7 %copy-done.10 = f32[2,128]{1,0:T(2,128)S(1)} copy-done((f32[2,128]{1,0:T(2,128)S(1)}, f32[2,128]{1,0:T(2,128)}, u32[]{:S(2)}) %copy-start.10) | copy-done | bytes 1048
  43.0 0.7 %copy-done.12 = s32[2,128]{1,0:T(2,128)S(1)} copy-done((s32[2,128]{1,0:T(2,128)S(1)}, s32[2,128]{1,0:T(2,128)}, u32[]{:S(2)}) %copy-start.12) | copy-done | bytes 1048
  43.6 9.1 %force.1 = (f32[3,8,128]{2,1,0:T(8,128)}, f32[3,8,128]{2,1,0:T(8,128)}) custom-call(s32[8,27]{1,0:T(8,128)S(1)} %copy-done.8, s32[2,128]{1,0:T(2,128)S(1)} %copy-done.12, f32[8,128,128]{2,1,0:T(8,128)S(1)} %copy-done.1, s32[256,128]{1,0:T(8,128)S(1)} %get-tuple-element.31.orders, f32[8,8,128]{2,1,0:T(8,128)S(1)} %copy-done.5, f32[2,48,128]{2,1,0:T(8,128)S(1)} %copy-done.3, ...), custom_call_target="tpu_custom_call" | custom-call | flops 1000000000 | bytes 1000 | tf_op jit(solution)/shard_map/force/pallas_call | solution.py:618
  (15 shorter events, 0.0 us)
Async XLA Ops:
  2.3 11.9 %copy-start.6 = (s32[8,27]{1,0:T(8,128)S(1)}, s32[8,27]{1,0:T(8,128)}, u32[]{:S(2)}) copy-start(s32[8,27]{1,0:T(8,128)} %pair_source.5) | copy-start | bytes 2596
  2.3 11.9 %copy-start.15 = (s32[8,27]{1,0:T(8,128)S(1)}, s32[8,27]{1,0:T(8,128)}, u32[]{:S(2)}) copy-start(s32[8,27]{1,0:T(8,128)} %pair_shift.3) | copy-start | bytes 2596
  2.3 11.9 %copy-start.17 = (s32[16,2]{0,1:T(2,128)S(1)}, s32[16,2]{0,1:T(2,128)}, u32[]{:S(2)}) copy-start(s32[16,2]{0,1:T(2,128)} %param.23) | copy-start | bytes 388
  2.3 11.9 %copy-start.21 = (f32[8,16,128]{2,1,0:T(8,128)S(1)}, f32[8,16,128]{2,1,0:T(8,128)}, u32[]{:S(2)}) copy-start(f32[8,16,128]{2,1,0:T(8,128)} %get-tuple-element.21.own) | copy-start | bytes 196612
  2.3 11.8 %all-to-all-start = ((f32[16,24,128]{2,1,0:T(8,128)}), f32[16,24,128]{2,1,0:T(8,128)S(1)}, u32[]{:S(2)}, u32[]{:S(2)}) async-start(f32[16,24,128]{2,1,0:T(8,128)} %get-tuple-element.23), calls=%async_computation | async-start | bytes 393216 | tf_op jit(solution)/shard_map/all_to_all | solution.py:536
  8.5 5.6 %collective-permute-start = (f32[2,12,128]{2,1,0:T(8,128)}, f32[2,12,128]{2,1,0:T(8,128)S(1)}, u32[]{:S(2)}, u32[]{:S(2)}) collective-permute-start(f32[2,12,128]{2,1,0:T(8,128)} %get-tuple-element.24), channel_id=1, source_target_pairs={{0,16},{16,0},{1,17},{17,1},{2,18},{18,2},{3,19},{19,3},{4,20},{20... | collective-permute-start | bytes 36872 | tf_op jit(solution)/shard_map/ppermute | solution.py:543
  10.0 0.8 %copy-start.20 = (f32[8,16,128]{2,1,0:T(8,128)S(1)}, f32[8,16,128]{2,1,0:T(8,128)}, u32[]{:S(2)}) copy-start(f32[8,16,128]{2,1,0:T(8,128)} %get-tuple-element.21.own) | copy-start | bytes 196612
  14.1 12.7 %copy-start.18 = (f32[8,32,128]{2,1,0:T(8,128)}, f32[8,32,128]{2,1,0:T(8,128)S(1)}, u32[]{:S(2)}) copy-start(f32[8,32,128]{2,1,0:T(8,128)S(1)} %get-tuple-element.25.bundle) | copy-start | bytes 393220
  14.1 12.7 %copy-start.13 = (f32[2,12,128]{2,1,0:T(8,128)}, f32[2,12,128]{2,1,0:T(8,128)S(1)}, u32[]{:S(2)}) copy-start(f32[2,12,128]{2,1,0:T(8,128)S(1)} %collective-permute-done.border) | copy-start | bytes 36868
  19.7 0.6 %copy-start.23 = (f32[2,8,128]{2,1,0:T(8,128)}, f32[2,8,128]{2,1,0:T(8,128)S(1)}, u32[]{:S(2)}) copy-start(f32[2,8,128]{2,1,0:T(8,128)S(1)} %get-tuple-element.28.densities) | copy-start | bytes 24580
  20.3 18.6 %all-to-all-start.1 = ((f32[16,2,128]{2,1,0:T(2,128)}), f32[16,2,128]{2,1,0:T(2,128)S(1)}, u32[]{:S(2)}, u32[]{:S(2)}) async-start(f32[16,2,128]{2,1,0:T(2,128)} %get-tuple-element.34), calls=%async_computation.1 | async-start | bytes 32768 | tf_op jit(solution)/shard_map/all_to_all | solution.py:536
  26.4 12.1 %collective-permute-start.1 = (f32[2,128]{1,0:T(2,128)}, f32[2,128]{1,0:T(2,128)S(1)}, u32[]{:S(2)}, u32[]{:S(2)}) collective-permute-start(f32[2,128]{1,0:T(2,128)} %get-tuple-element.35), channel_id=1, source_target_pairs={{0,16},{16,0},{1,17},{17,1},{2,18},{18,2},{3,19},{19,3},{4,20},{20... | collective-permute-start | bytes 3080 | tf_op jit(solution)/shard_map/ppermute | solution.py:543
  26.8 0.7 %copy-start.7 = (s32[8,27]{1,0:T(8,128)S(1)}, s32[8,27]{1,0:T(8,128)}, u32[]{:S(2)}) copy-start(s32[8,27]{1,0:T(8,128)} %pair_source.5) | copy-start | bytes 2596
  27.5 0.7 %copy-start.14 = (f32[2,12,128]{2,1,0:T(8,128)S(1)}, f32[2,12,128]{2,1,0:T(8,128)}, u32[]{:S(2)}) copy-start(f32[2,12,128]{2,1,0:T(8,128)} %copy-done.13) | copy-start | bytes 36868
  28.2 0.7 %copy-start.16 = (s32[8,27]{1,0:T(8,128)S(1)}, s32[8,27]{1,0:T(8,128)}, u32[]{:S(2)}) copy-start(s32[8,27]{1,0:T(8,128)} %pair_shift.3) | copy-start | bytes 2596
  28.9 0.9 %copy-start.19 = (f32[8,32,128]{2,1,0:T(8,128)S(1)}, f32[8,32,128]{2,1,0:T(8,128)}, u32[]{:S(2)}) copy-start(f32[8,32,128]{2,1,0:T(8,128)} %copy-done.18) | copy-start | bytes 393220
  29.8 0.8 %copy-start.22 = (f32[8,16,128]{2,1,0:T(8,128)S(1)}, f32[8,16,128]{2,1,0:T(8,128)}, u32[]{:S(2)}) copy-start(f32[8,16,128]{2,1,0:T(8,128)} %get-tuple-element.21.own) | copy-start | bytes 196612
  30.6 0.7 %copy-start.24 = (f32[2,8,128]{2,1,0:T(8,128)S(1)}, f32[2,8,128]{2,1,0:T(8,128)}, u32[]{:S(2)}) copy-start(f32[2,8,128]{2,1,0:T(8,128)} %copy-done.23) | copy-start | bytes 24580
  35.8 0.8 %copy-start = (f32[8,128,128]{2,1,0:T(8,128)}, f32[8,128,128]{2,1,0:T(8,128)S(1)}, u32[]{:S(2)}) copy-start(f32[8,128,128]{2,1,0:T(8,128)S(1)} %get-tuple-element.30.columns) | copy-start | bytes 1572868
  36.6 0.6 %copy-start.2 = (f32[2,48,128]{2,1,0:T(8,128)}, f32[2,48,128]{2,1,0:T(8,128)S(1)}, u32[]{:S(2)}) copy-start(f32[2,48,128]{2,1,0:T(8,128)S(1)} %get-tuple-element.33.traits) | copy-start | bytes 147460
  37.2 0.6 %copy-start.4 = (f32[8,8,128]{2,1,0:T(8,128)}, f32[8,8,128]{2,1,0:T(8,128)S(1)}, u32[]{:S(2)}) copy-start(f32[8,8,128]{2,1,0:T(8,128)S(1)} %get-tuple-element.32.last) | copy-start | bytes 98308
  37.9 0.6 %copy-start.11 = (s32[2,128]{1,0:T(2,128)}, s32[2,128]{1,0:T(2,128)S(1)}, u32[]{:S(2)}) copy-start(s32[2,128]{1,0:T(2,128)S(1)} %get-tuple-element.29.starts) | copy-start | bytes 3076
  38.4 0.6 %copy-start.9 = (f32[2,128]{1,0:T(2,128)}, f32[2,128]{1,0:T(2,128)S(1)}, u32[]{:S(2)}) copy-start(f32[2,128]{1,0:T(2,128)S(1)} %collective-permute-done.1.new_border) | copy-start | bytes 3076
  39.0 1.0 %copy-start.1 = (f32[8,128,128]{2,1,0:T(8,128)S(1)}, f32[8,128,128]{2,1,0:T(8,128)}, u32[]{:S(2)}) copy-start(f32[8,128,128]{2,1,0:T(8,128)} %copy-done) | copy-start | bytes 1572868
  40.0 0.8 %copy-start.3 = (f32[2,48,128]{2,1,0:T(8,128)S(1)}, f32[2,48,128]{2,1,0:T(8,128)}, u32[]{:S(2)}) copy-start(f32[2,48,128]{2,1,0:T(8,128)} %copy-done.2) | copy-start | bytes 147460
  40.8 0.8 %copy-start.5 = (f32[8,8,128]{2,1,0:T(8,128)S(1)}, f32[8,8,128]{2,1,0:T(8,128)}, u32[]{:S(2)}) copy-start(f32[8,8,128]{2,1,0:T(8,128)} %copy-done.4) | copy-start | bytes 98308
  41.6 0.7 %copy-start.8 = (s32[8,27]{1,0:T(8,128)S(1)}, s32[8,27]{1,0:T(8,128)}, u32[]{:S(2)}) copy-start(s32[8,27]{1,0:T(8,128)} %pair_source.5) | copy-start | bytes 2596
  42.3 0.7 %copy-start.10 = (f32[2,128]{1,0:T(2,128)S(1)}, f32[2,128]{1,0:T(2,128)}, u32[]{:S(2)}) copy-start(f32[2,128]{1,0:T(2,128)} %copy-done.9) | copy-start | bytes 3076
  43.0 0.7 %copy-start.12 = (s32[2,128]{1,0:T(2,128)S(1)}, s32[2,128]{1,0:T(2,128)}, u32[]{:S(2)}) copy-start(s32[2,128]{1,0:T(2,128)} %copy-done.11) | copy-start | bytes 3076
